TPU v7x, 256 devices: a whole 4x4x8 slice. The times are simulated.
256 devices in a mesh: aux: 4 (over y), shell: 64 (over z, x, core).
Axes of the slice: x: 4, y: 4, z: 8, core: 2. Of those that a mesh axis runs over, the one named last changes fastest.
Arguments:
- three_center: bfloat16 [64, 40, 4, 128, 128], P('shell', None, 'aux'), may hold values from -6 to 6
- occupied: bfloat16 [8192, 384], P('shell'), may hold values from -0.01953125 to 0.01953125
- tile_blocks: int32 [4, 64, 40], P('aux', 'shell'), may hold values from 0 to 63, as said below
Outputs:
- exchange_matrix: float32 [8192, 8192], P('shell', 'aux')
Inputs may be any that keep to these rules, and one draw needn't show every extreme that they name: In each row tile_blocks[a, g] the 40 mu blocks are distinct, and the first is g itself.
All inputs are finite; a program needn't handle non-finite values.
Results may differ from a plain program's by a relative error of at most 0.014.
Values may be sent and summed in bfloat16 or wider, within the bound.
A program may use at most 64 MiB of HBM per device.

v0:
```python
import math

import jax
import jax.numpy as jnp
from jax import lax
from jax.sharding import PartitionSpec as P


def body(three_center, occupied, tile_blocks):
    blk_dev, tile_blk, aux_dev, block_rows, _ = three_center.shape
    occ_width = occupied.shape[1]
    block_count = blk_dev * lax.axis_size("shell")
    targets = tile_blocks[0]
    lam_index = jnp.broadcast_to(jnp.arange(blk_dev, dtype=jnp.int32)[:, None], targets.shape)
    sending = jnp.zeros((blk_dev, block_count, aux_dev, block_rows, block_rows), jnp.bfloat16)
    sending = sending.at[lam_index, targets].set(three_center)
    arrived = lax.all_to_all(sending, "shell", split_axis=1, concat_axis=0, tiled=True)
    empty = jnp.zeros((blk_dev, aux_dev, block_rows, occ_width), jnp.float32)
    running_sum = empty
    shard_rows = lax.all_gather(occupied, "shell", axis=0, tiled=True)
    pieces_count = shard_rows.shape[0] // block_rows
    group_size = math.gcd(pieces_count, 8)
    orbital = shard_rows.reshape(pieces_count // group_size, group_size, block_rows, occ_width)

    def inner_step(running, step_index):
        blocks_here = lax.dynamic_slice_in_dim(arrived, step_index * group_size, group_size, 0)
        halfway = jnp.einsum(
            "kmaxl,kli->kmaxi", blocks_here, orbital[step_index], preferred_element_type=jnp.float32
        ).astype(jnp.bfloat16)
        return (running + jnp.sum(halfway, axis=0, dtype=jnp.float32), None)

    running_sum, _ = lax.scan(
        inner_step, running_sum, jnp.arange(pieces_count // group_size, dtype=jnp.int32)
    )
    fitted = running_sum.astype(jnp.bfloat16)
    shard_rows = lax.all_gather(fitted, "shell", axis=0, tiled=True)
    pieces_count = shard_rows.shape[0]
    product_rows = jnp.einsum(
        "maxi,nayi->mxny", fitted, shard_rows, preferred_element_type=jnp.float32
    )
    partial_value = product_rows.reshape(blk_dev * block_rows, pieces_count * block_rows)
    return lax.psum_scatter(partial_value, "aux", scatter_dimension=1, tiled=True)


def solution(mesh):
    return jax.shard_map(
        body,
        mesh=mesh,
        in_specs=(P("shell", None, "aux", None, None), P("shell", None), P("aux", "shell", None)),
        out_specs=P("shell", "aux"),
        check_vma=False,
    )
```

profile of v0, /device:TPU:1, one launch (start us, length us, event | category | flops | bytes accessed | tf_op | source)
XLA Modules:
  0.0 281.9 jit_solution(17042173356296673598)
XLA Ops:
  6.5 0.0 copy-start
  6.5 0.0 all-gather.3.cloned.1.call-start
  6.5 0.7 all-gather.3.cloned.1.call-update
  7.3 0.7 compare_select_fusion
  7.9 1.9 broadcast.22
  9.8 0.0 copy-done
  9.8 6.5 %scatter_fusion = bf16[64,128,128]{2,1,0:T(8,128)(2,1)} fusion(bf16[64,128,128]{2,1,0:T(8,128)(2,1)} %broadcast.22, s32[40]{0:T(128)S(1)} %fusion.9, bf16[40,128,128]{2,1,0:T(8,128)(2,1)S(1)} %bitcast.37), kind=kCustom, calls=%fused_computation | custom fusion | bytes 3932320 | tf_op jit(solution)/shard_map/scatter | solution.py:16
  16.3 13.0 %all-to-all-start = ((bf16[1,64,1,128,128]{4,3,2,0,1:T(8,128)(2,1)}), bf16[1,64,1,128,128]{4,3,2,0,1:T(8,128)(2,1)S(1)}, u32[]{:S(2)}, u32[]{:S(2)}) async-start(bf16[1,64,1,128,128]{4,3,2,0,1:T(8,128)(2,1)} %bitcast.4), calls=%async_computation | async-start | bytes 4194304 | tf_op jit(solution)/shard_map/all_to_all | solution.py:17
  29.4 0.0 all-gather.5.cloned.1.call-start
  29.4 57.6 %all-to-all-done = bf16[1,64,1,128,128]{4,3,2,0,1:T(8,128)(2,1)S(1)} async-done(((bf16[1,64,1,128,128]{4,3,2,0,1:T(8,128)(2,1)}), bf16[1,64,1,128,128]{4,3,2,0,1:T(8,128)(2,1)S(1)}, u32[]{:S(2)}, u32[]{:S(2)}) %all-to-all-start) | async-done | bytes 2097184 | tf_op jit(solution)/shard_map/all_to_all | solution.py:17
  87.1 17.3 %all-gather.3.cloned.1.call-done = bf16[8192,384]{1,0:T(8,128)(2,1)} async-done(((bf16[128,384]{1,0:T(8,128)(2,1)}), bf16[8192,384]{1,0:T(8,128)(2,1)}) %all-gather.3.cloned.1.call-update) | async-done | bytes 6291472 | tf_op jit(solution)/shard_map/all_gather | solution.py:20
  104.4 37.8 %while.11 = (s32[]{:T(128)}, f32[1,1,128,384]{3,2,1,0:T(8,128)S(1)}, s32[8]{0:T(128)S(1)}, bf16[64,1,1,128,128]{4,3,0,2,1:T(8,128)(2,1)S(1)}, bf16[8,8,128,384]{...) while((s32[]{:T(128)}, f32[1,1,128,384]{3,2,1,0:T(8,128)S(1)}, ...), condition=%wide.region_3.4_spmd.clone, body=%wide.region_1.3_spmd.clone.sunk | while | flops 101892104 | bytes 1835211 | solution.py:32
  104.4 0.6 dynamic_slice.28
  107.5 1.5 convert_reduce_fusion.2
  109.0 0.1 bitcast_add_fusion.2
  109.1 0.6 dynamic_slice.28
  112.3 1.5 convert_reduce_fusion.2
  113.8 0.1 bitcast_add_fusion.2
  113.8 0.6 dynamic_slice.28
  117.0 1.5 convert_reduce_fusion.2
  118.5 0.1 bitcast_add_fusion.2
  118.6 0.6 dynamic_slice.28
  121.7 1.5 convert_reduce_fusion.2
  123.2 0.1 bitcast_add_fusion.2
  123.3 0.6 dynamic_slice.28
  126.4 1.5 convert_reduce_fusion.2
  127.9 0.1 bitcast_add_fusion.2
  128.0 0.6 dynamic_slice.28
  131.2 1.5 convert_reduce_fusion.2
  132.7 0.1 bitcast_add_fusion.2
  132.7 0.6 dynamic_slice.28
  135.9 1.5 convert_reduce_fusion.2
  137.4 0.1 bitcast_add_fusion.2
  137.5 0.6 dynamic_slice.28
  140.6 1.5 convert_reduce_fusion.2
  142.1 0.1 bitcast_add_fusion.2
  142.2 0.7 convert_element_type.11
  142.8 0.0 all-gather.5.cloned.1.call-update
  142.9 0.0 reduce-scatter.2.cloned.1.call-start
  142.9 79.8 %all-gather.5.cloned.1.call-done = bf16[64,1,128,384]{3,2,1,0:T(8,128)(2,1)} async-done(((bf16[1,1,128,384]{3,2,1,0:T(8,128)(2,1)}), bf16[64,1,128,384]{3,2,1,0:T(8,128)(2,1)}) %all-gather.5.cloned.1.call-update) | async-done | bytes 6291472 | tf_op jit(solution)/shard_map/all_gather | solution.py:36
  222.7 6.9 %fusion.7 = f32[128,8192]{1,0:T(8,128)} fusion(bf16[8192,384]{1,0:T(8,128)(2,1)} %bitcast.34, bf16[1,1,128,384]{3,2,1,0:T(8,128)(2,1)} %convert_element_type.11), kind=kOutput, calls=%fused_computation.9 | convolution fusion | flops 805306368 | bytes 10584064 | tf_op jit(solution)/shard_map/maxi,nayi->mxny/dot_general | solution.py:38
  229.6 0.0 reduce-scatter.2.cloned.1.call-update
  229.6 45.8 %reduce-scatter.2.cloned.1.call-done = f32[128,2048]{1,0:T(8,128)} async-done(((f32[128,8192]{1,0:T(8,128)}), f32[128,2048]{1,0:T(8,128)}) %reduce-scatter.2.cloned.1.call-update) | async-done | bytes 1048592 | tf_op jit(solution)/shard_map/reduce_scatter | solution.py:42
  (4 shorter events, 0.0 us)
Async XLA Ops:
  6.5 3.3 %copy-start = (bf16[1,40,1,128,128]{4,3,2,1,0:T(8,128)(2,1)S(1)}, bf16[1,40,1,128,128]{4,3,2,1,0:T(8,128)(2,1)}, u32[]{:S(2)}) copy-start(bf16[1,40,1,128,128]{4,3,2,1,0:T(8,128)(2,1)} %param.5) | copy-start | bytes 3932164
  6.5 97.9 %all-gather.3.cloned.1.call-start = ((), (), s32[]{:S(2)}) async-start(), calls=%async_computation.2 | async-start | bytes 6389760 | tf_op jit(solution)/shard_map/all_gather | solution.py:20
  16.3 70.7 %all-to-all-start = ((bf16[1,64,1,128,128]{4,3,2,0,1:T(8,128)(2,1)}), bf16[1,64,1,128,128]{4,3,2,0,1:T(8,128)(2,1)S(1)}, u32[]{:S(2)}, u32[]{:S(2)}) async-start(bf16[1,64,1,128,128]{4,3,2,0,1:T(8,128)(2,1)} %bitcast.4), calls=%async_computation | async-start | bytes 4194304 | tf_op jit(solution)/shard_map/all_to_all | solution.py:17
  29.4 193.3 %all-gather.5.cloned.1.call-start = ((), (), s32[]{:S(2)}) async-start(), calls=%async_computation.3 | async-start | bytes 6389760 | tf_op jit(solution)/shard_map/all_gather | solution.py:36
  142.9 132.5 %reduce-scatter.2.cloned.1.call-start = ((), (), s32[]{:S(2)}) async-start(), calls=%async_computation.4 | async-start | bytes 5242880 | tf_op jit(solution)/shard_map/reduce_scatter | solution.py:42
Sparse Core Ops, SparseCore 0:
  10.1 94.2 all-gather.2
  143.0 79.6 all-gather.4
  229.7 45.5 reduce-scatter.1
where the time goes:
time: 283 us; the launch traced here: 282 us
  waiting for transfers between devices  201 us (71%)
  loops' own time  20.2 us (7%)
  matrix products  19 us (7%)
  local copies, waits for them, and re-layouts  13.6 us (5%)
  starting transfers between devices  13.1 us (5%)
  between operations  13.1 us (5%)
    all_gather x1, waiting for transfers between devices, body(): shard_rows = lax.all_gather(fitted, 'shell', axis=0, tiled=True)  79.8 us
    all_to_all x1, waiting for transfers between devices, body(): lax.all_to_all(sending, 'shell', split_axis=1, concat_axis=0, tiled=True)  57.6 us
    reduce_scatter x1, waiting for transfers between devices, body(): lax.psum_scatter(partial_value, 'aux', scatter_dimension=1, tiled=True)  45.8 us
    another operation x1, loops' own time, body(): lax.scan(inner_step, running_sum, jnp.arange(pieces_count // group_size,...  20.2 us
    all_gather x1, waiting for transfers between devices, body(): shard_rows = lax.all_gather(occupied, 'shell', axis=0, tiled=True)  17.3 us
    all_to_all x1, starting transfers between devices, body(): lax.all_to_all(sending, 'shell', split_axis=1, concat_axis=0, tiled=True)  13 us
    dot_general x8, matrix products, inner_step(): jnp.einsum('kmaxl,kli->kmaxi', blocks_here, orbital[step_index], preferre...  12 us
    dot_general x1, matrix products, body(): jnp.einsum('maxi,nayi->mxny', fitted, shard_rows, preferred_element_type=...  6.93 us
  transfers between devices with their start and end apart: 4, of which 4 were waited for; matrix products, arithmetic and copies ran while one was open for 3% of the time, Pallas kernels for 0%

commit v1 on v0

v1 whole, which is shorter than its diff:
```python
import jax
import jax.numpy as jnp
from jax import lax
from jax.experimental import pallas as pl
from jax.experimental.pallas import tpu as pltpu
from jax.sharding import PartitionSpec as P

MESH = pl.DeviceIdType.MESH
BLK = 128
OCC = 384
TILES = 40
NY, NZ, NX = 4, 8, 4

WINDOW = [(dz, dx, e) for dz in range(2) for dx in range(2) for e in range(2)]
PARTS = [(2 * k, 2 * j) for k in range(4) for j in range(2)]
ROWS = [(dx, e) for dx in range(NX) for e in range(2)]


def greeted():
    out = set()
    for dz, dx, e in WINDOW:
        out.add((0, dz, dx, e))
        out.add((0, -dz % NZ, -dx % NX, e))
    for dz, dx in PARTS:
        out.add((0, dz, dx, 0))
    for dz in range(NZ):
        out.add((0, dz, 0, 0))
    for dy in range(NY):
        for dx, e in ROWS:
            out.add((dy, 0, dx, e))
    out.discard((0, 0, 0, 0))
    return sorted(out)


def kernel(
    slots_ref, tiles_ref, occ_ref, out_ref,
    dense, tiles_in, occ_in, part, part_in, rows, cols, pair, pair_in,
    s_tile, r_tile, s_occ, r_occ, s_part, r_part, s_row, r_row, s_col, r_col, s_pair, r_pair,
):
    y = lax.axis_index("aux")
    shell = lax.axis_index("shell")
    z, x, c = shell // (2 * NX), (shell // 2) % NX, shell % 2

    def device(dy, zz, xx, cc):
        return ((y + dy) % NY, zz * (2 * NX) + xx * 2 + cc)

    def near(dy=0, dz=0, dx=0, e=0):
        return device(dy, (z + dz) % NZ, (x + dx) % NX, (c + e) % 2)

    def copy(src, dst, send, recv, to):
        return pltpu.make_async_remote_copy(
            src_ref=src, dst_ref=dst, send_sem=send, recv_sem=recv, device_id=to, device_id_type=MESH
        )

    peers = greeted()
    barrier = pltpu.get_barrier_semaphore()
    for dy, dz, dx, e in peers:
        pl.semaphore_signal(barrier, inc=1, device_id=near(dy, dz, dx, e), device_id_type=MESH)

    def target(dz, dx, e):
        tc = (c + e) % 2
        sign = 1 - 2 * tc
        return (z - sign * dz + NZ) % NZ, (x - sign * dx + NX) % NX, tc

    for s, (dz, dx, e) in enumerate(WINDOW):
        tz, tx, tc = target(dz, dx, e)
        to = tiles_in.at[0] if s == 0 else dense.at[s]

        def fill(i, carry, to=to, tz=tz, tx=tx, tc=tc):
            k, j = i // 2, i % 2
            block = ((tz + 2 * k) % NZ) * (2 * NX) + ((tx + 2 * j) % NX) * 2 + tc
            slot = slots_ref[block]
            held = tiles_ref[jnp.maximum(slot - 1, 0)]
            to[i] = jnp.where(slot > 0, held, jnp.zeros_like(held))
            return carry

        lax.fori_loop(0, 8, fill, 0)
    occ_in[0] = occ_ref[...]

    pl.semaphore_wait(barrier, len(peers))

    sends = []
    for s, w in enumerate(WINDOW):
        if s:
            tz, tx, tc = target(*w)
            cp = copy(occ_ref, occ_in.at[s], s_occ.at[s], r_occ.at[s], device(0, tz, tx, tc))
            cp.start()
            sends.append(cp)
    first = []
    for s, w in enumerate(WINDOW):
        if s:
            tz, tx, tc = target(*w)
            cp = copy(dense.at[s], tiles_in.at[s], s_tile.at[s], r_tile.at[s], device(0, tz, tx, tc))
            cp.start()
            first.append(cp)
    for cp in sends + first:
        cp.wait_recv()

    def work(i, carry):
        lhs = jnp.concatenate([tiles_in[s, i] for s in range(8)], axis=1)
        rhs = occ_in[...].reshape(8 * BLK, OCC)
        part[i] = jnp.dot(lhs, rhs, preferred_element_type=jnp.float32).astype(jnp.bfloat16)
        return carry

    lax.fori_loop(0, 8, work, 0)
    second = []
    for i, (dz, dx) in enumerate(PARTS):
        if i:
            cp = copy(part.at[i], part_in.at[i], s_part.at[i], r_part.at[i], near(0, dz, dx, 0))
            cp.start()
            second.append(cp)
    total = part[0].astype(jnp.float32)
    for i, cp in enumerate(second):
        cp.wait_recv()
        total = total + part_in[i + 1].astype(jnp.float32)
    rows[0] = total.astype(jnp.bfloat16)
    cols[z] = total.astype(jnp.bfloat16)

    third = []
    for dz in range(1, NZ):
        cp = copy(rows.at[0], cols.at[z], s_col.at[dz], r_col.at[dz], near(0, dz, 0, 0))
        cp.start()
        third.append(cp)
    across = []
    for r, (dx, e) in enumerate(ROWS):
        if r:
            cp = copy(rows.at[0], rows.at[r], s_row.at[r], r_row.at[r], near(0, 0, -dx, e))
            cp.start()
            across.append(cp)
    for cp in across:
        cp.wait_recv()
    for dz in range(1, NZ):
        copy(rows.at[0], cols.at[(z - dz + NZ) % NZ], s_col.at[dz], r_col.at[dz], near(0, dz, 0, 0)).wait_recv()

    fourth = []
    for dy in (2, 1, 3, 0):
        ty = (y + dy) % NY
        rhs = cols[pl.ds(2 * ty, 2)].reshape(2 * BLK, OCC)

        def product(r, carry, dy=dy, rhs=rhs):
            both = lax.dot_general(
                rows[r], rhs, (((1,), (1,)), ((), ())), preferred_element_type=jnp.float32
            )
            pair[dy * 8 + r] = both.astype(jnp.bfloat16)
            return carry

        lax.fori_loop(0, 8, product, 0)
        for r, (dx, e) in enumerate(ROWS):
            if dy or r:
                i = dy * 8 + r
                cp = copy(pair.at[i], pair_in.at[i], s_pair.at[i], r_pair.at[i], near(dy, 0, dx, e))
                cp.start()
                fourth.append(cp)
    for cp in fourth:
        cp.wait_recv()
    for r, (dx, e) in enumerate(ROWS):
        own = pair[0] if r == 0 else pair_in[r]
        value = own.astype(jnp.float32)
        for dy in range(1, NY):
            value = value + pair_in[dy * 8 + r].astype(jnp.float32)
        at = ((x - dx + NX) % NX) * 2 + (c + e) % 2
        for zz in range(2):
            lane = pl.multiple_of(zz * (8 * BLK) + at * BLK, BLK)
            out_ref[:, pl.ds(lane, BLK)] = value[:, zz * BLK:(zz + 1) * BLK]
    for cp in sends + first + second + third + across + fourth:
        cp.wait_send()


def body(three_center, occupied, tile_blocks):
    tiles = three_center.reshape(TILES, BLK, BLK)
    targets = tile_blocks.reshape(TILES)
    hit = targets[None, :] == jnp.arange(NZ * NX * 2, dtype=jnp.int32)[:, None]
    slots = jnp.sum(jnp.where(hit, jnp.arange(1, TILES + 1, dtype=jnp.int32)[None, :], 0), axis=1)
    vmem = pl.BlockSpec(memory_space=pltpu.VMEM)
    bf16 = jnp.bfloat16
    dma = pltpu.SemaphoreType.DMA
    return pl.pallas_call(
        kernel,
        out_shape=jax.ShapeDtypeStruct((BLK, 2048), jnp.float32),
        in_specs=[pl.BlockSpec(memory_space=pltpu.SMEM), vmem, vmem],
        out_specs=vmem,
        scratch_shapes=[
            pltpu.VMEM((8, 8, BLK, BLK), bf16),
            pltpu.VMEM((8, 8, BLK, BLK), bf16),
            pltpu.VMEM((8, BLK, OCC), bf16),
            pltpu.VMEM((8, BLK, OCC), bf16),
            pltpu.VMEM((8, BLK, OCC), bf16),
            pltpu.VMEM((8, BLK, OCC), bf16),
            pltpu.VMEM((8, BLK, OCC), bf16),
            pltpu.VMEM((32, BLK, 2 * BLK), bf16),
            pltpu.VMEM((32, BLK, 2 * BLK), bf16),
            dma((8,)), dma((8,)), dma((8,)), dma((8,)), dma((8,)), dma((8,)),
            dma((8,)), dma((8,)), dma((8,)), dma((8,)), dma((32,)), dma((32,)),
        ],
        compiler_params=pltpu.CompilerParams(
            collective_id=0, has_side_effects=True, vmem_limit_bytes=48 * 1024 * 1024
        ),
        cost_estimate=pl.CostEstimate(flops=1_700_000_000, bytes_accessed=3_000_000, transcendentals=0),
    )(slots, tiles, occupied)


def solution(mesh):
    return jax.shard_map(
        body,
        mesh=mesh,
        in_specs=(P("shell", None, "aux", None, None), P("shell", None), P("aux", "shell", None)),
        out_specs=P("shell", "aux"),
        check_vma=False,
    )
```

time: 283 us -> 111 us (0.39)
  the two profiles are of different devices: /device:TPU:1 before, /device:TPU:197 now
where the time goes in v1:
time: 111 us
  Pallas kernels  107 us (96%)
  local copies, waits for them, and re-layouts  3.18 us (3%)
    pallas_call x1, Pallas kernels, body(): pl.pallas_call(kernel, out_shape=jax.ShapeDtypeStruct((BLK, 2048), jnp.fl...  107 us
    unnamed x5, local copies, waits for them, and re-layouts  3.18 us

profile of v1, /device:TPU:197, one launch (start us, length us, event | category | flops | bytes accessed | tf_op | source)
XLA Modules:
  0.0 110.5 jit_solution(4321115471046660347)
XLA Ops:
  0.0 0.7 select_reduce_fusion.slots_ref
  0.7 0.0 copy-start
  0.8 1.3 %copy-done = bf16[1,40,1,128,128]{4,3,2,1,0:T(8,128)(2,1)S(1)} copy-done((bf16[1,40,1,128,128]{4,3,2,1,0:T(8,128)(2,1)S(1)}, bf16[1,40,1,128,128]{4,3,2,1,0:T(8,128)(2,1)}, u32[]{:S(2)}) %copy-start) | copy-done | bytes 1310744
  2.1 0.0 copy-start.1
  2.1 0.9 copy-done.1
  3.0 106.6 %shard_map.37 = f32[128,2048]{1,0:T(8,128)S(1)} custom-call(s32[64]{0:T(128)S(1)} %select_reduce_fusion.slots_ref, bf16[40,128,128]{2,1,0:T(8,128)(2,1)S(1)} %bitcast.2, bf16[128,384]{1,0:T(8,128)(2,1)S(1)} %copy-done.1), custom_call_target="tpu_custom_call" | custom-call | flops 1700000000 | bytes 3000000 | tf_op jit(solution)/shard_map/pallas_call | solution.py:177
  109.6 1.0 copy.5
  (1 shorter events, 0.0 us)
Async XLA Ops:
  0.7 1.3 %copy-start = (bf16[1,40,1,128,128]{4,3,2,1,0:T(8,128)(2,1)S(1)}, bf16[1,40,1,128,128]{4,3,2,1,0:T(8,128)(2,1)}, u32[]{:S(2)}) copy-start(bf16[1,40,1,128,128]{4,3,2,1,0:T(8,128)(2,1)} %param.3) | copy-start | bytes 3932164
  2.1 0.9 copy-start.1

commit v2 on v1

v2 whole, which is shorter than its diff:
```python
import jax
import jax.numpy as jnp
from jax import lax
from jax.experimental import pallas as pl
from jax.experimental.pallas import tpu as pltpu
from jax.sharding import PartitionSpec as P

MESH = pl.DeviceIdType.MESH
BLK = 128
HALF = BLK // 2
OCC = 384
TILES = 40
NY, NZ, NX = 4, 8, 4

WINDOW = [(dz, dx, e) for dz in range(2) for dx in range(2) for e in range(2)]
ROWS = [(dx, e) for dx in range(NX) for e in range(2)]
ORDER = (2, 1, 3, 0)


def greeted():
    out = {(0, 0, 2, 0)}
    for dz, dx, e in WINDOW:
        out.add((0, dz, dx, e))
        out.add((0, -dz % NZ, -dx % NX, e))
    for dz in range(NZ):
        out.add((0, dz, 0, 0))
    for dy in range(NY):
        for dx, e in ROWS:
            out.add((dy, 0, dx, e))
    out.discard((0, 0, 0, 0))
    return sorted(out)


def kernel(
    slots_ref, tiles_hbm, occ_ref, out_ref,
    tiles_ref, dense, tiles_in, occ_in, own, part, part_in, mid, mid_in, rows, cols, pair, pair_in,
    s_load, s_tile, r_tile, s_occ, r_occ, s_part, r_part, s_mid, r_mid, s_row, r_row, s_col, r_col, s_pair, r_pair,
):
    y = lax.axis_index("aux")
    shell = lax.axis_index("shell")
    z, x, c = shell // (2 * NX), (shell // 2) % NX, shell % 2

    def device(dy, zz, xx, cc):
        return ((y + dy) % NY, zz * (2 * NX) + xx * 2 + cc)

    def near(dy=0, dz=0, dx=0, e=0):
        return device(dy, (z + dz) % NZ, (x + dx) % NX, (c + e) % 2)

    def copy(src, dst, send, recv, to):
        return pltpu.make_async_remote_copy(
            src_ref=src, dst_ref=dst, send_sem=send, recv_sem=recv, device_id=to, device_id_type=MESH
        )

    started = []
    load = pltpu.make_async_copy(tiles_hbm, tiles_ref, s_load)
    load.start()
    peers = greeted()
    barrier = pltpu.get_barrier_semaphore()
    for dy, dz, dx, e in peers:
        pl.semaphore_signal(barrier, inc=1, device_id=near(dy, dz, dx, e), device_id_type=MESH)

    def target(dz, dx, e):
        tc = (c + e) % 2
        sign = 1 - 2 * tc
        return (z - sign * dz + NZ) % NZ, (x - sign * dx + NX) % NX, tc

    def spread(k):
        def fill(i, carry):
            s, j = i // 2, i % 2
            tz, tx, tc = target(s // 4, (s // 2) % 2, s % 2)
            block = ((tz + 2 * k) % NZ) * (2 * NX) + ((tx + 2 * j) % NX) * 2 + tc
            slot = slots_ref[block]
            held = tiles_ref[jnp.maximum(slot - 1, 0)]
            dense[k, s, j] = jnp.where(slot > 0, held, jnp.zeros_like(held))
            return carry

        lax.fori_loop(0, 16, fill, 0)

    occ_in[0] = occ_ref[...]
    load.wait()
    spread(ORDER[0])
    pl.semaphore_wait(barrier, len(peers))
    for s, w in enumerate(WINDOW):
        if s:
            cp = copy(occ_ref, occ_in.at[s], s_occ.at[s], r_occ.at[s], device(0, *target(*w)))
            cp.start()
            started.append(cp)
    orbital = list(started)
    arriving = {}
    for k in ORDER:
        if k != ORDER[0]:
            spread(k)
        arriving[k] = []
        for s, w in enumerate(WINDOW):
            if s:
                cp = copy(dense.at[k, s], tiles_in.at[k, s], s_tile.at[k, s], r_tile.at[k, s], device(0, *target(*w)))
                cp.start()
                arriving[k].append(cp)
        started += arriving[k]
    for cp in orbital:
        cp.wait_recv()

    facing = {}
    for k in ORDER:
        for cp in arriving[k]:
            cp.wait_recv()
        lhs = jnp.concatenate(
            [
                jnp.concatenate([dense[k, 0, j]] + [tiles_in[k, s, j] for s in range(1, 8)], axis=1)
                for j in range(2)
            ],
            axis=0,
        )
        both = jnp.dot(lhs, occ_in[...].reshape(8 * BLK, OCC), preferred_element_type=jnp.float32)
        own[k] = both[:BLK]
        part[k] = both[BLK:].astype(jnp.bfloat16)
        cp = copy(part.at[k], part_in.at[k], s_part.at[k], r_part.at[k], near(0, 0, 2, 0))
        cp.start()
        started.append(cp)
        facing[k] = cp
    along = []
    for k in ORDER:
        facing[k].wait_recv()
        own[k] += part_in[k].astype(jnp.float32)
        if k:
            mid[k] = own[k].astype(jnp.bfloat16)
            cp = copy(mid.at[k], mid_in.at[k], s_mid.at[k], r_mid.at[k], near(0, 2 * k, 0, 0))
            cp.start()
            started.append(cp)
            along.append((k, cp))
    total = own[0]
    for k, cp in along:
        cp.wait_recv()
        total = total + mid_in[k].astype(jnp.float32)
    fitted = total.astype(jnp.bfloat16)
    rows[0] = fitted
    cols[0, z] = fitted[:HALF]
    cols[1, z] = fitted[HALF:]

    across = []
    for r, (dx, e) in enumerate(ROWS):
        if r:
            cp = copy(rows.at[0], rows.at[r], s_row.at[r], r_row.at[r], near(0, 0, -dx, e))
            cp.start()
            across.append(cp)
    started += across
    for h in range(2):
        for dz in (4, 3, 5, 2, 6, 1, 7):
            half = rows.at[0, pl.ds(h * HALF, HALF)]
            cp = copy(half, cols.at[h, z], s_col.at[h, dz], r_col.at[h, dz], near(0, dz, 0, 0))
            cp.start()
            started.append(cp)
    for cp in across:
        cp.wait_recv()

    last = []
    for h in range(2):
        for dz in range(1, NZ):
            there = cols.at[h, (z - dz + NZ) % NZ]
            copy(there, there, s_col.at[h, dz], r_col.at[h, dz], near(0, dz, 0, 0)).wait_recv()
        rhs = cols[h].reshape(NZ * HALF, OCC)
        for r, (dx, e) in enumerate(ROWS):
            block = lax.dot_general(
                rows[r], rhs, (((1,), (1,)), ((), ())), preferred_element_type=jnp.float32
            ).astype(jnp.bfloat16)
            for a in range(NY):
                pair[h, a, r] = block[:, a * BLK:(a + 1) * BLK]
            for dy in (2, 1, 3, 0):
                if dy or r:
                    cp = copy(
                        pair.at[h, (y + dy) % NY, r], pair_in.at[h, dy, r],
                        s_pair.at[h, dy, r], r_pair.at[h, dy, r], near(dy, 0, dx, e),
                    )
                    cp.start()
                    last.append(cp)
    started += last
    for cp in last:
        cp.wait_recv()
    for r, (dx, e) in enumerate(ROWS):
        halves = []
        for h in range(2):
            value = (pair[h, y, 0] if r == 0 else pair_in[h, 0, r]).astype(jnp.float32)
            for dy in range(1, NY):
                value = value + pair_in[h, dy, r].astype(jnp.float32)
            halves.append(value)
        at = ((x - dx + NX) % NX) * 2 + (c + e) % 2
        for zz in range(2):
            lane = pl.multiple_of(zz * (8 * BLK) + at * BLK, BLK)
            out_ref[:, pl.ds(lane, BLK)] = jnp.concatenate(
                [v[:, zz * HALF:(zz + 1) * HALF] for v in halves], axis=1
            )
    for cp in started:
        cp.wait_send()


def body(three_center, occupied, tile_blocks):
    tiles = three_center.reshape(TILES, BLK, BLK)
    targets = tile_blocks.reshape(TILES)
    hit = targets[None, :] == jnp.arange(NZ * NX * 2, dtype=jnp.int32)[:, None]
    slots = jnp.sum(jnp.where(hit, jnp.arange(1, TILES + 1, dtype=jnp.int32)[None, :], 0), axis=1)
    vmem = pl.BlockSpec(memory_space=pltpu.VMEM)
    bf16, f32 = jnp.bfloat16, jnp.float32
    dma = pltpu.SemaphoreType.DMA
    return pl.pallas_call(
        kernel,
        out_shape=jax.ShapeDtypeStruct((BLK, 2048), f32),
        in_specs=[pl.BlockSpec(memory_space=pltpu.SMEM), pl.BlockSpec(memory_space=pl.ANY), vmem],
        out_specs=vmem,
        scratch_shapes=[
            pltpu.VMEM((TILES, BLK, BLK), bf16),
            pltpu.VMEM((4, 8, 2, BLK, BLK), bf16),
            pltpu.VMEM((4, 8, 2, BLK, BLK), bf16),
            pltpu.VMEM((8, BLK, OCC), bf16),
            pltpu.VMEM((4, BLK, OCC), f32),
            pltpu.VMEM((4, BLK, OCC), bf16),
            pltpu.VMEM((4, BLK, OCC), bf16),
            pltpu.VMEM((4, BLK, OCC), bf16),
            pltpu.VMEM((4, BLK, OCC), bf16),
            pltpu.VMEM((8, BLK, OCC), bf16),
            pltpu.VMEM((2, NZ, HALF, OCC), bf16),
            pltpu.VMEM((2, NY, 8, BLK, BLK), bf16),
            pltpu.VMEM((2, NY, 8, BLK, BLK), bf16),
            dma(()),
            dma((4, 8)), dma((4, 8)), dma((8,)), dma((8,)), dma((4,)), dma((4,)), dma((4,)), dma((4,)),
            dma((8,)), dma((8,)), dma((2, 8)), dma((2, 8)), dma((2, NY, 8)), dma((2, NY, 8)),
        ],
        compiler_params=pltpu.CompilerParams(
            collective_id=0, has_side_effects=True, vmem_limit_bytes=60 * 1024 * 1024
        ),
        cost_estimate=pl.CostEstimate(flops=1_700_000_000, bytes_accessed=3_000_000, transcendentals=0),
    )(slots, tiles, occupied)


def solution(mesh):
    return jax.shard_map(
        body,
        mesh=mesh,
        in_specs=(P("shell", None, "aux", None, None), P("shell", None), P("aux", "shell", None)),
        out_specs=P("shell", "aux"),
        check_vma=False,
    )
```

time: 111 us -> 89.5 us (0.81)
  the two profiles are of different devices: /device:TPU:197 before, /device:TPU:1 now
where the time goes in v2:
time: 89.5 us; the launch traced here: 88.6 us
  Pallas kernels  85.1 us (95%)
  local copies, waits for them, and re-layouts  2.3 us (3%)
  other arithmetic  1.26 us (1%)
    pallas_call x1, Pallas kernels, body(): pl.pallas_call(kernel, out_shape=jax.ShapeDtypeStruct((BLK, 2048), f32),...  85.1 us
    unnamed x1, local copies, waits for them, and re-layouts  2.3 us

profile of v2, /device:TPU:1, one launch (start us, length us, event | category | flops | bytes accessed | tf_op | source)
XLA Modules:
  0.0 88.6 jit_solution(4304005270756729029)
XLA Ops:
  0.0 1.3 %select_reduce_fusion.slots_ref = s32[64]{0:T(128)} fusion(s32[40]{0:T(128)S(1)} %iota_add_fusion, s32[40]{0:T(128)} %bitcast.3), kind=kLoop, calls=%fused_computation | loop fusion | flops 7616 | bytes 576 | tf_op jit(solution)/shard_map/reduce_sum | solution.py:200
  1.3 85.1 %shard_map.37 = f32[128,2048]{1,0:T(8,128)} custom-call(s32[64]{0:T(128)} %select_reduce_fusion.slots_ref, bf16[40,128,128]{2,1,0:T(8,128)(2,1)} %bitcast.2, bf16[128,384]{1,0:T(8,128)(2,1)} %occ_ref.1), custom_call_target="tpu_custom_call" | custom-call | flops 1700000000 | bytes 3000000 | tf_op jit(solution)/shard_map/pallas_call | solution.py:204
  86.4 2.3 %copy.5 = f32[128,2048]{1,0:T(8,128)} copy(f32[128,2048]{1,0:T(8,128)} %shard_map.37) | data formatting | bytes 2097152
  (1 shorter events, 0.0 us)

commit v3 on v2

v3 whole, which is shorter than its diff:
```python
import jax
import jax.numpy as jnp
from jax import lax
from jax.experimental import pallas as pl
from jax.experimental.pallas import tpu as pltpu
from jax.sharding import PartitionSpec as P

MESH = pl.DeviceIdType.MESH
BLK = 128
OCC = 384
TILES = 40
NY, NZ, NX = 4, 8, 4

WINDOW = [(dz, dx, e) for dz in range(2) for dx in range(2) for e in range(2)]
ROWS = [(dx, e) for dx in range(NX) for e in range(2)]
ORDER = (2, 1, 3, 0)
CHUNKS = (0, 1, 3, 2)


def greeted():
    out = set()
    for dz, dx, e in WINDOW:
        out.add((0, dz, dx, e))
        out.add((0, -dz % NZ, -dx % NX, e))
    for dz in range(NZ):
        out.add((0, dz, 0, 0))
    for dy in range(NY):
        out.add((dy, 0, 0, 0))
    for dx, e in ROWS:
        out.add((0, 0, dx, e))
    out.discard((0, 0, 0, 0))
    return sorted(out)


def kernel(
    slots_ref, tiles_hbm, occ_hbm, out_ref,
    tiles_ref, dense, tiles_in, occ_in, own, part, part_in, mid, mid_in, rows, cols, pair, pair_in, done, done_in,
    mirror_in, twin_in, twin, twin_done, twin_mirror,
    s_load, s_load_occ, s_tile, r_tile, s_occ, r_occ, s_part, r_part, s_mid, r_mid, s_row, r_row, s_col, r_col, s_pair, r_pair,
    s_done, r_done, s_mirror, r_mirror, s_twin, r_twin, s_out, r_out, s_back, r_back,
):
    y = lax.axis_index("aux")
    shell = lax.axis_index("shell")
    z, x, c = shell // (2 * NX), (shell // 2) % NX, shell % 2

    def device(dy, zz, xx, cc):
        return ((y + dy) % NY, zz * (2 * NX) + xx * 2 + cc)

    def near(dy=0, dz=0, dx=0, e=0):
        return device(dy, (z + dz) % NZ, (x + dx) % NX, (c + e) % 2)

    def copy(src, dst, send, recv, to):
        return pltpu.make_async_remote_copy(
            src_ref=src, dst_ref=dst, send_sem=send, recv_sem=recv, device_id=to, device_id_type=MESH
        )

    started = []
    load = pltpu.make_async_copy(tiles_hbm, tiles_ref, s_load)
    load.start()
    load_occ = pltpu.make_async_copy(occ_hbm, occ_in.at[0], s_load_occ)
    load_occ.start()
    peers = greeted()
    barrier = pltpu.get_barrier_semaphore()
    for dy, dz, dx, e in peers:
        pl.semaphore_signal(barrier, inc=1, device_id=near(dy, dz, dx, e), device_id_type=MESH)
    zp, zs = z // 2, z % 2
    home = y == zp
    chosen = jnp.where(home, z, 2 * y + jnp.where(y > zp, zs, 1 - zs))
    other = jnp.where(home, z + 1 - 2 * zs, 2 * y + jnp.where(y > zp, 1 - zs, zs))
    shell_of = lambda zz: zz * (2 * NX) + x * 2 + c
    pl.semaphore_signal(barrier, inc=1, device_id=(zp, shell_of(other)), device_id_type=MESH)

    def target(dz, dx, e):
        tc = (c + e) % 2
        sign = 1 - 2 * tc
        return (z - sign * dz + NZ) % NZ, (x - sign * dx + NX) % NX, tc

    def spread(k):
        def fill(i, carry):
            s, j = i // 2, i % 2
            tz, tx, tc = target(s // 4, (s // 2) % 2, s % 2)
            block = ((tz + 2 * k) % NZ) * (2 * NX) + ((tx + 2 * j) % NX) * 2 + tc
            slot = slots_ref[block]
            held = tiles_ref[jnp.maximum(slot - 1, 0)]
            dense[k, s, j] = jnp.where(slot > 0, held, jnp.zeros_like(held))
            return carry

        lax.fori_loop(0, 16, fill, 0)

    load_occ.wait()
    pl.semaphore_wait(barrier, len(peers) + 1)
    for s, w in enumerate(WINDOW):
        if s:
            cp = copy(occ_in.at[0], occ_in.at[s], s_occ.at[s], r_occ.at[s], device(0, *target(*w)))
            cp.start()
            started.append(cp)
    orbital = list(started)
    arriving = {}
    load.wait()
    for k in ORDER:
        spread(k)
        arriving[k] = []
        for s, w in enumerate(WINDOW):
            if s:
                cp = copy(dense.at[k, s], tiles_in.at[k, s], s_tile.at[k, s], r_tile.at[k, s], device(0, *target(*w)))
                cp.start()
                arriving[k].append(cp)
        started += arriving[k]
    for cp in orbital:
        cp.wait_recv()

    facing = {}
    for k in ORDER:
        for cp in arriving[k]:
            cp.wait_recv()
        lhs = jnp.concatenate(
            [
                jnp.concatenate([dense[k, 0, j]] + [tiles_in[k, s, j] for s in range(1, 8)], axis=1)
                for j in range(2)
            ],
            axis=0,
        )
        both = jnp.dot(lhs, occ_in[...].reshape(8 * BLK, OCC), preferred_element_type=jnp.float32)
        own[k] = both[:BLK]
        part[k] = both[BLK:].astype(jnp.bfloat16)
        cp = copy(part.at[k], part_in.at[k], s_part.at[k], r_part.at[k], near(0, 0, 2, 0))
        cp.start()
        started.append(cp)
        facing[k] = cp
    along = []
    for k in ORDER:
        facing[k].wait_recv()
        own[k] += part_in[k].astype(jnp.float32)
        if k:
            mid[k] = own[k].astype(jnp.bfloat16)
            cp = copy(mid.at[k], mid_in.at[k], s_mid.at[k], r_mid.at[k], near(0, 2 * k, 0, 0))
            cp.start()
            started.append(cp)
            along.append((k, cp))
    total = own[0]
    for k, cp in along:
        cp.wait_recv()
        total = total + mid_in[k].astype(jnp.float32)
    fitted = total.astype(jnp.bfloat16)
    rows[0] = fitted
    cols[zp] = fitted

    across = {}
    for r in (1, 2, 3, 6, 7, 4, 5):
        dx, e = ROWS[r]
        cp = copy(rows.at[0], rows.at[r], s_row.at[r], r_row.at[r], near(0, 0, -dx, e))
        cp.start()
        across[r] = cp
        started.append(cp)
    up = []
    for d in (2, 1, 3, 0):
        there = (zp + d) % 4
        if d:
            tz = 2 * there + jnp.where(there < zp, zs, 1 - zs)
            cp = copy(rows.at[0], cols.at[zp], s_col.at[d], r_col.at[d], (y, shell_of(tz)))
        else:
            cp = copy(rows.at[0], cols.at[4], s_col.at[d], r_col.at[d], (y, shell_of(z + 1 - 2 * zs)))
        cp.start()
        started.append(cp)
        up.append(d)
    for d in up:
        there = cols.at[(zp - d + 4) % 4] if d else cols.at[4]
        copy(there, there, s_col.at[d], r_col.at[d], (y, shell_of(z + 1 - 2 * zs))).wait_recv()

    shares = {}
    for q in CHUNKS:
        for r in (2 * q, 2 * q + 1):
            if r:
                across[r].wait_recv()
        block = lax.dot_general(
            rows[2 * q:2 * q + 2].reshape(2 * BLK, OCC), cols[...].reshape(5 * BLK, OCC),
            (((1,), (1,)), ((), ())), preferred_element_type=jnp.float32,
        ).astype(jnp.bfloat16)
        for a in range(5):
            for i in range(2):
                pair[a, 2 * q + i] = block[i * BLK:(i + 1) * BLK, a * BLK:(a + 1) * BLK]
        shares[q] = []
        for dy in (2, 1, 3):
            two = pl.ds(2 * q, 2)
            cp = copy(
                pair.at[(y + dy) % NY, two], pair_in.at[dy, two], s_pair.at[dy, q], r_pair.at[dy, q], near(dy, 0, 0, 0)
            )
            cp.start()
            shares[q].append(cp)
        started += shares[q]
    half = pl.ds(2 * zs, 4)
    to_home = (zp - y + NY) % NY
    twin_send = copy(pair.at[4, half], twin_in.at[to_home], s_twin, r_twin.at[to_home], (zp, shell))

    @pl.when(jnp.logical_not(home))
    def _():
        twin_send.start()

    mirror = {}
    given = {}
    for q in CHUNKS:
        for cp in shares[q]:
            cp.wait_recv()
        two = pl.ds(2 * q, 2)
        value = pair[y, two].astype(jnp.float32)
        for dy in range(1, NY):
            value = value + pair_in[dy, two].astype(jnp.float32)
        done[two] = value.astype(jnp.bfloat16)
        mirror[q] = copy(done.at[two], mirror_in.at[two], s_mirror.at[q], r_mirror.at[q], (zp, shell_of(chosen)))

        @pl.when(jnp.logical_not(home))
        def _(q=q):
            mirror[q].start()

        for r in (2 * q, 2 * q + 1):
            if r:
                dx, e = ROWS[r]
                cp = copy(done.at[r], done_in.at[r], s_done.at[r], r_done.at[r], near(0, 0, dx, e))
                cp.start()
                given[r] = cp
    started += list(given.values())

    def neighbour(i):
        r = 2 * zs + i
        return (y, z * (2 * NX) + ((x + r // 2) % NX) * 2 + (c + r % 2) % 2)

    back = copy(twin_done, twin_mirror, s_back, r_back, (zp, shell_of(z + 1 - 2 * zs)))
    turned = [copy(twin_done.at[i], twin.at[i], s_out.at[i], r_out.at[i], neighbour(i)) for i in range(4)]

    @pl.when(home)
    def _():
        for dy in range(1, NY):
            copy(pair.at[4, half], twin_in.at[dy], s_twin, r_twin.at[dy], (zp, shell)).wait_recv()
        value = pair[4, half].astype(jnp.float32)
        for dy in range(1, NY):
            value = value + twin_in[dy].astype(jnp.float32)
        twin_done[...] = value.astype(jnp.bfloat16)
        back.start()
        for i in range(1, 4):
            turned[i].start()

        @pl.when(zs == 1)
        def _():
            turned[0].start()

    def place(zz, dx, e, value):
        at = ((x + dx + NX) % NX) * 2 + (c + e) % 2
        lane = pl.multiple_of(zz * (8 * BLK) + at * BLK, BLK)
        out_ref[:, pl.ds(lane, BLK)] = value.astype(jnp.float32)

    for q in CHUNKS:
        for r in (2 * q, 2 * q + 1):
            dx, e = ROWS[r]
            if r:
                given[r].wait_recv()
            place(chosen % 2, -dx, e, done_in[r] if r else done[0])

    @pl.when(jnp.logical_not(home))
    def _():
        for q in CHUNKS:
            mirror[q].wait_recv()
            for r in (2 * q, 2 * q + 1):
                dx, e = ROWS[r]
                place(other % 2, dx, e, mirror_in[r].astype(jnp.float32).T)
        twin_send.wait_send()
        for q in CHUNKS:
            mirror[q].wait_send()

    @pl.when(home)
    def _():
        back.wait_recv()
        for i in range(4):
            r = 2 * (1 - zs) + i
            place(1 - zs, r // 2, r % 2, twin_mirror[i].astype(jnp.float32).T)
        for i in range(1, 4):
            turned[i].wait_recv()
            r = 2 * zs + i
            place(1 - zs, -(r // 2), r % 2, twin[i])

        @pl.when(zs == 1)
        def _():
            turned[0].wait_recv()
            place(1 - zs, -1, 0, twin[0])
            turned[0].wait_send()

        @pl.when(zs == 0)
        def _():
            place(1 - zs, 0, 0, twin_done[0])

        back.wait_send()
        for i in range(1, 4):
            turned[i].wait_send()

    for cp in started:
        cp.wait_send()


def body(three_center, occupied, tile_blocks):
    tiles = three_center.reshape(TILES, BLK, BLK)
    targets = tile_blocks.reshape(TILES)
    hit = targets[None, :] == jnp.arange(NZ * NX * 2, dtype=jnp.int32)[:, None]
    slots = jnp.sum(jnp.where(hit, jnp.arange(1, TILES + 1, dtype=jnp.int32)[None, :], 0), axis=1)
    hbm = pl.BlockSpec(memory_space=pltpu.HBM)
    bf16, f32 = jnp.bfloat16, jnp.float32
    dma = pltpu.SemaphoreType.DMA
    return pl.pallas_call(
        kernel,
        out_shape=jax.ShapeDtypeStruct((BLK, 2048), f32),
        in_specs=[pl.BlockSpec(memory_space=pltpu.SMEM), hbm, hbm],
        out_specs=pl.BlockSpec(memory_space=pltpu.VMEM),
        scratch_shapes=[
            pltpu.VMEM((TILES, BLK, BLK), bf16),
            pltpu.VMEM((4, 8, 2, BLK, BLK), bf16),
            pltpu.VMEM((4, 8, 2, BLK, BLK), bf16),
            pltpu.VMEM((8, BLK, OCC), bf16),
            pltpu.VMEM((4, BLK, OCC), f32),
            pltpu.VMEM((4, BLK, OCC), bf16),
            pltpu.VMEM((4, BLK, OCC), bf16),
            pltpu.VMEM((4, BLK, OCC), bf16),
            pltpu.VMEM((4, BLK, OCC), bf16),
            pltpu.VMEM((8, BLK, OCC), bf16),
            pltpu.VMEM((5, BLK, OCC), bf16),
            pltpu.VMEM((5, 8, BLK, BLK), bf16),
            pltpu.VMEM((4, 8, BLK, BLK), bf16),
            pltpu.VMEM((8, BLK, BLK), bf16),
            pltpu.VMEM((8, BLK, BLK), bf16),
            pltpu.VMEM((8, BLK, BLK), bf16),
            pltpu.VMEM((4, 4, BLK, BLK), bf16),
            pltpu.VMEM((4, BLK, BLK), bf16),
            pltpu.VMEM((4, BLK, BLK), bf16),
            pltpu.VMEM((4, BLK, BLK), bf16),
            dma(()), dma(()),
            dma((4, 8)), dma((4, 8)), dma((8,)), dma((8,)), dma((4,)), dma((4,)), dma((4,)), dma((4,)),
            dma((8,)), dma((8,)), dma((4,)), dma((4,)), dma((4, 4)), dma((4, 4)),
            dma((8,)), dma((8,)), dma((4,)), dma((4,)), dma(()), dma((4,)), dma((4,)), dma((4,)), dma(()), dma(()),
        ],
        compiler_params=pltpu.CompilerParams(
            collective_id=0, has_side_effects=True, vmem_limit_bytes=52 * 1024 * 1024
        ),
        cost_estimate=pl.CostEstimate(flops=1_700_000_000, bytes_accessed=3_000_000, transcendentals=0),
    )(slots, tiles, occupied)


def solution(mesh):
    return jax.shard_map(
        body,
        mesh=mesh,
        in_specs=(P("shell", None, "aux", None, None), P("shell", None), P("aux", "shell", None)),
        out_specs=P("shell", "aux"),
        check_vma=False,
    )
```

time: 89.5 us -> 86.9 us (0.971)
  the two profiles are of different devices: /device:TPU:1 before, /device:TPU:16 now
where the time goes in v3:
time: 86.9 us; the launch traced here: 86.8 us
  Pallas kernels  84.2 us (97%)
  local copies, waits for them, and re-layouts  1.86 us (2%)
    pallas_call x1, Pallas kernels, body(): pl.pallas_call(kernel, out_shape=jax.ShapeDtypeStruct((BLK, 2048), f32),...  84.2 us
    unnamed x3, local copies, waits for them, and re-layouts  1.86 us

profile of v3, /device:TPU:16, one launch (start us, length us, event | category | flops | bytes accessed | tf_op | source)
XLA Modules:
  0.0 86.8 jit_solution(14746960337392518413)
XLA Ops:
  0.0 0.7 select_reduce_fusion.slots_ref
  0.7 0.0 copy-start
  0.8 0.9 %copy-done = bf16[128,384]{1,0:T(8,128)(2,1)S(1)} copy-done((bf16[128,384]{1,0:T(8,128)(2,1)S(1)}, bf16[128,384]{1,0:T(8,128)(2,1)}, u32[]{:S(2)}) %copy-start) | copy-done | bytes 98328
  1.6 84.2 %shard_map.37 = f32[128,2048]{1,0:T(8,128)S(1)} custom-call(s32[64]{0:T(128)S(1)} %select_reduce_fusion.slots_ref, bf16[40,128,128]{2,1,0:T(8,128)(2,1)} %bitcast.2, bf16[128,384]{1,0:T(8,128)(2,1)S(1)} %copy-done), custom_call_target="tpu_custom_call" | custom-call | flops 1700000000 | bytes 3000000 | tf_op jit(solution)/shard_map/pallas_call | solution.py:306
  85.8 1.0 %copy.5 = f32[128,2048]{1,0:T(8,128)} copy(f32[128,2048]{1,0:T(8,128)S(1)} %shard_map.37) | data formatting | bytes 2097152
  (1 shorter events, 0.0 us)
Async XLA Ops:
  0.7 0.9 %copy-start = (bf16[128,384]{1,0:T(8,128)(2,1)S(1)}, bf16[128,384]{1,0:T(8,128)(2,1)}, u32[]{:S(2)}) copy-start(bf16[128,384]{1,0:T(8,128)(2,1)} %occ_hbm.1) | copy-start | bytes 294916

commit v4 on v3

--- a/solution.py
+++ b/solution.py
@@ -13,8 +13,12 @@
 
 WINDOW = [(dz, dx, e) for dz in range(2) for dx in range(2) for e in range(2)]
 ROWS = [(dx, e) for dx in range(NX) for e in range(2)]
-ORDER = (2, 1, 3, 0)
-CHUNKS = (0, 1, 3, 2)
+GROUPS = (((1, 2), (1, 1)), ((1, 3), (1, 0)), ((0, 2), (0, 1)), ((0, 3),), ((0, 0),))
+FIRST = (0, 2, 4, 6, 7)
+AHEAD = 5
+CHUNKS = (0, 1, 2, 3)
+RELAYED = (0, 1)
+FORWARD = {2: 0, 3: 1}
 
 
 def greeted():
@@ -34,10 +38,10 @@
 
 def kernel(
     slots_ref, tiles_hbm, occ_hbm, out_ref,
-    tiles_ref, dense, tiles_in, occ_in, own, part, part_in, mid, mid_in, rows, cols, pair, pair_in, done, done_in,
-    mirror_in, twin_in, twin, twin_done, twin_mirror,
+    tiles_ref, dense, tiles_in, occ_in, part, part_in, mid, mid_in, rows, cols, pair, pair_in, done, done_in,
+    mirror_in, relay, twin_in, twin, twin_done, twin_mirror,
     s_load, s_load_occ, s_tile, r_tile, s_occ, r_occ, s_part, r_part, s_mid, r_mid, s_row, r_row, s_col, r_col, s_pair, r_pair,
-    s_done, r_done, s_mirror, r_mirror, s_twin, r_twin, s_out, r_out, s_back, r_back,
+    s_done, r_done, s_mirror, r_mirror, s_relay, r_relay, s_twin, r_twin, s_out, r_out, s_back, r_back,
 ):
     y = lax.axis_index("aux")
     shell = lax.axis_index("shell")
@@ -75,17 +79,18 @@
         sign = 1 - 2 * tc
         return (z - sign * dz + NZ) % NZ, (x - sign * dx + NX) % NX, tc
 
-    def spread(k):
-        def fill(i, carry):
-            s, j = i // 2, i % 2
-            tz, tx, tc = target(s // 4, (s // 2) % 2, s % 2)
-            block = ((tz + 2 * k) % NZ) * (2 * NX) + ((tx + 2 * j) % NX) * 2 + tc
-            slot = slots_ref[block]
-            held = tiles_ref[jnp.maximum(slot - 1, 0)]
-            dense[k, s, j] = jnp.where(slot > 0, held, jnp.zeros_like(held))
-            return carry
-
-        lax.fori_loop(0, 16, fill, 0)
+    def spread(g):
+        for n, (j, k) in enumerate(GROUPS[g]):
+
+            def fill(s, carry, n=FIRST[g] + n, j=j, k=k):
+                tz, tx, tc = target(s // 4, (s // 2) % 2, s % 2)
+                block = ((tz + 2 * k) % NZ) * (2 * NX) + ((tx + 2 * j) % NX) * 2 + tc
+                slot = slots_ref[block]
+                held = tiles_ref[jnp.maximum(slot - 1, 0)]
+                dense[s, n] = jnp.where(slot > 0, held, jnp.zeros_like(held))
+                return carry
+
+            lax.fori_loop(0, 8, fill, 0)
 
     load_occ.wait()
     pl.semaphore_wait(barrier, len(peers) + 1)
@@ -97,47 +102,57 @@
     orbital = list(started)
     arriving = {}
     load.wait()
-    for k in ORDER:
-        spread(k)
-        arriving[k] = []
+
+    def leave(g):
+        here = pl.ds(FIRST[g], len(GROUPS[g]))
+        arriving[g] = []
         for s, w in enumerate(WINDOW):
             if s:
-                cp = copy(dense.at[k, s], tiles_in.at[k, s], s_tile.at[k, s], r_tile.at[k, s], device(0, *target(*w)))
+                cp = copy(dense.at[s, here], tiles_in.at[s, here], s_tile.at[g, s], r_tile.at[g, s], device(0, *target(*w)))
                 cp.start()
-                arriving[k].append(cp)
-        started += arriving[k]
+                arriving[g].append(cp)
+
+    for g in range(len(GROUPS)):
+        spread(g)
+        if g < AHEAD:
+            leave(g)
     for cp in orbital:
         cp.wait_recv()
 
     facing = {}
-    for k in ORDER:
-        for cp in arriving[k]:
+    along = []
+    for g, group in enumerate(GROUPS):
+        for cp in arriving[g]:
             cp.wait_recv()
         lhs = jnp.concatenate(
             [
-                jnp.concatenate([dense[k, 0, j]] + [tiles_in[k, s, j] for s in range(1, 8)], axis=1)
-                for j in range(2)
+                jnp.concatenate([dense[0, n]] + [tiles_in[s, n] for s in range(1, 8)], axis=1)
+                for n in range(FIRST[g], FIRST[g] + len(group))
             ],
             axis=0,
         )
         both = jnp.dot(lhs, occ_in[...].reshape(8 * BLK, OCC), preferred_element_type=jnp.float32)
-        own[k] = both[:BLK]
-        part[k] = both[BLK:].astype(jnp.bfloat16)
-        cp = copy(part.at[k], part_in.at[k], s_part.at[k], r_part.at[k], near(0, 0, 2, 0))
-        cp.start()
-        started.append(cp)
-        facing[k] = cp
-    along = []
-    for k in ORDER:
-        facing[k].wait_recv()
-        own[k] += part_in[k].astype(jnp.float32)
-        if k:
-            mid[k] = own[k].astype(jnp.bfloat16)
-            cp = copy(mid.at[k], mid_in.at[k], s_mid.at[k], r_mid.at[k], near(0, 2 * k, 0, 0))
+        for n, (j, k) in enumerate(group):
+            value = both[n * BLK:(n + 1) * BLK]
+            if j:
+                part[k] = value.astype(jnp.bfloat16)
+                cp = copy(part.at[k], part_in.at[k], s_part.at[k], r_part.at[k], near(0, 0, 2, 0))
+                facing[k] = cp
+            else:
+                facing[k].wait_recv()
+                value = value + part_in[k].astype(jnp.float32)
+                if k == 0:
+                    total = value
+                    continue
+                mid[k] = value.astype(jnp.bfloat16)
+                cp = copy(mid.at[k], mid_in.at[k], s_mid.at[k], r_mid.at[k], near(0, 2 * k, 0, 0))
+                along.append((k, cp))
             cp.start()
             started.append(cp)
-            along.append((k, cp))
-    total = own[0]
+        for cp in arriving[g]:
+            cp.wait_send()
+        if g + AHEAD < len(GROUPS):
+            leave(g + AHEAD)
     for k, cp in along:
         cp.wait_recv()
         total = total + mid_in[k].astype(jnp.float32)
@@ -146,13 +161,12 @@
     cols[zp] = fitted
 
     across = {}
-    for r in (1, 2, 3, 6, 7, 4, 5):
+    for r in (1, 2, 3, 4, 5, 6, 7):
         dx, e = ROWS[r]
         cp = copy(rows.at[0], rows.at[r], s_row.at[r], r_row.at[r], near(0, 0, -dx, e))
         cp.start()
         across[r] = cp
         started.append(cp)
-    up = []
     for d in (2, 1, 3, 0):
         there = (zp + d) % 4
         if d:
@@ -162,55 +176,70 @@
             cp = copy(rows.at[0], cols.at[4], s_col.at[d], r_col.at[d], (y, shell_of(z + 1 - 2 * zs)))
         cp.start()
         started.append(cp)
-        up.append(d)
-    for d in up:
+    def wait_column(d):
         there = cols.at[(zp - d + 4) % 4] if d else cols.at[4]
         copy(there, there, s_col.at[d], r_col.at[d], (y, shell_of(z + 1 - 2 * zs))).wait_recv()
 
-    shares = {}
-    for q in CHUNKS:
+    def share(dy, q):
+        two = pl.ds(2 * q, 2)
+        return copy(pair.at[(y + dy) % NY, two], pair_in.at[dy, two], s_pair.at[dy, q], r_pair.at[dy, q], near(dy, 0, 0, 0))
+
+    def product(q, rhs):
+        return lax.dot_general(
+            rows[2 * q:2 * q + 2].reshape(2 * BLK, OCC), rhs,
+            (((1,), (1,)), ((), ())), preferred_element_type=jnp.float32,
+        ).astype(jnp.bfloat16)
+
+    def issue(q):
         for r in (2 * q, 2 * q + 1):
             if r:
                 across[r].wait_recv()
-        block = lax.dot_general(
-            rows[2 * q:2 * q + 2].reshape(2 * BLK, OCC), cols[...].reshape(5 * BLK, OCC),
-            (((1,), (1,)), ((), ())), preferred_element_type=jnp.float32,
-        ).astype(jnp.bfloat16)
+        if q == 0:
+            for d in (0, 1, 3, 2):
+                a = (zp - d + 4) % 4
+                if d:
+                    wait_column(d)
+                pair[a, 0:2] = product(q, cols[a]).reshape(2, BLK, BLK)
+                dy = (a - y + NY) % NY
+
+                @pl.when(a != y)
+                def _(dy=dy):
+                    share(dy, 0).start()
+
+            wait_column(0)
+            pair[4, 0:2] = product(q, cols[4]).reshape(2, BLK, BLK)
+            return
+        block = product(q, cols[...].reshape(5 * BLK, OCC))
         for a in range(5):
             for i in range(2):
                 pair[a, 2 * q + i] = block[i * BLK:(i + 1) * BLK, a * BLK:(a + 1) * BLK]
-        shares[q] = []
         for dy in (2, 1, 3):
-            two = pl.ds(2 * q, 2)
-            cp = copy(
-                pair.at[(y + dy) % NY, two], pair_in.at[dy, two], s_pair.at[dy, q], r_pair.at[dy, q], near(dy, 0, 0, 0)
-            )
-            cp.start()
-            shares[q].append(cp)
-        started += shares[q]
+            share(dy, q).start()
+
     half = pl.ds(2 * zs, 4)
     to_home = (zp - y + NY) % NY
     twin_send = copy(pair.at[4, half], twin_in.at[to_home], s_twin, r_twin.at[to_home], (zp, shell))
 
-    @pl.when(jnp.logical_not(home))
-    def _():
-        twin_send.start()
-
     mirror = {}
+    forward = {}
     given = {}
-    for q in CHUNKS:
-        for cp in shares[q]:
-            cp.wait_recv()
+
+    def finish(q):
+        for dy in (2, 1, 3):
+            share(dy, q).wait_recv()
         two = pl.ds(2 * q, 2)
         value = pair[y, two].astype(jnp.float32)
         for dy in range(1, NY):
             value = value + pair_in[dy, two].astype(jnp.float32)
         done[two] = value.astype(jnp.bfloat16)
         mirror[q] = copy(done.at[two], mirror_in.at[two], s_mirror.at[q], r_mirror.at[q], (zp, shell_of(chosen)))
+        leaving = mirror[q]
+        if q in RELAYED:
+            leaving = copy(done.at[two], relay.at[zp, two], s_mirror.at[q], r_relay.at[zp, q], (y, shell_of(chosen)))
 
         @pl.when(jnp.logical_not(home))
-        def _(q=q):
-            mirror[q].start()
+        def _(leaving=leaving):
+            leaving.start()
 
         for r in (2 * q, 2 * q + 1):
             if r:
@@ -218,6 +247,38 @@
                 cp = copy(done.at[r], done_in.at[r], s_done.at[r], r_done.at[r], near(0, 0, dx, e))
                 cp.start()
                 given[r] = cp
+        if q in FORWARD:
+            was = FORWARD[q]
+            forward[was] = []
+            for d in range(1, 4):
+                there = (zp + d) % 4
+                rest = pl.ds(2 * was, 2)
+                forward[was].append(
+                    copy(relay.at[there, rest], mirror_in.at[rest], s_relay.at[d, was], r_mirror.at[was], (there, shell))
+                )
+
+            @pl.when(home)
+            def _(was=was):
+                for d, cp in enumerate(forward[was]):
+                    there = (zp + d + 1) % 4
+                    come = relay.at[there, pl.ds(2 * was, 2)]
+                    copy(come, come, s_relay.at[d + 1, was], r_relay.at[there, was], (there, shell)).wait_recv()
+                    cp.start()
+
+    for q in range(4):
+        issue(q)
+        if q == 2:
+            @pl.when(jnp.logical_not(home))
+            def _():
+                twin_send.start()
+        if q:
+            finish(q - 1)
+            for dy in (2, 1, 3):
+                share(dy, q - 1).wait_send()
+    finish(3)
+    for dy in (2, 1, 3):
+        share(dy, 3).wait_send()
+
     started += list(given.values())
 
     def neighbour(i):
@@ -290,6 +351,9 @@
         back.wait_send()
         for i in range(1, 4):
             turned[i].wait_send()
+        for was in RELAYED:
+            for cp in forward[was]:
+                cp.wait_send()
 
     for cp in started:
         cp.wait_send()
@@ -310,10 +374,9 @@
         out_specs=pl.BlockSpec(memory_space=pltpu.VMEM),
         scratch_shapes=[
             pltpu.VMEM((TILES, BLK, BLK), bf16),
-            pltpu.VMEM((4, 8, 2, BLK, BLK), bf16),
-            pltpu.VMEM((4, 8, 2, BLK, BLK), bf16),
+            pltpu.VMEM((8, 8, BLK, BLK), bf16),
+            pltpu.VMEM((8, 8, BLK, BLK), bf16),
             pltpu.VMEM((8, BLK, OCC), bf16),
-            pltpu.VMEM((4, BLK, OCC), f32),
             pltpu.VMEM((4, BLK, OCC), bf16),
             pltpu.VMEM((4, BLK, OCC), bf16),
             pltpu.VMEM((4, BLK, OCC), bf16),
@@ -326,13 +389,14 @@
             pltpu.VMEM((8, BLK, BLK), bf16),
             pltpu.VMEM((8, BLK, BLK), bf16),
             pltpu.VMEM((4, 4, BLK, BLK), bf16),
+            pltpu.VMEM((4, 4, BLK, BLK), bf16),
             pltpu.VMEM((4, BLK, BLK), bf16),
             pltpu.VMEM((4, BLK, BLK), bf16),
             pltpu.VMEM((4, BLK, BLK), bf16),
             dma(()), dma(()),
-            dma((4, 8)), dma((4, 8)), dma((8,)), dma((8,)), dma((4,)), dma((4,)), dma((4,)), dma((4,)),
+            dma((5, 8)), dma((5, 8)), dma((8,)), dma((8,)), dma((4,)), dma((4,)), dma((4,)), dma((4,)),
             dma((8,)), dma((8,)), dma((4,)), dma((4,)), dma((4, 4)), dma((4, 4)),
-            dma((8,)), dma((8,)), dma((4,)), dma((4,)), dma(()), dma((4,)), dma((4,)), dma((4,)), dma(()), dma(()),
+            dma((8,)), dma((8,)), dma((4,)), dma((4,)), dma((4, 2)), dma((4, 2)), dma(()), dma((4,)), dma((4,)), dma((4,)), dma(()), dma(()),
         ],
         compiler_params=pltpu.CompilerParams(
             collective_id=0, has_side_effects=True, vmem_limit_bytes=52 * 1024 * 1024

time: 86.9 us -> 82.9 us (0.954)
  the two profiles are of different devices: /device:TPU:16 before, /device:TPU:1 now
where the time goes in v4:
time: 82.9 us; the launch traced here: 82.8 us
  Pallas kernels  80.2 us (97%)
  local copies, waits for them, and re-layouts  1.86 us (2%)
    pallas_call x1, Pallas kernels, body(): pl.pallas_call(kernel, out_shape=jax.ShapeDtypeStruct((BLK, 2048), f32),...  80.2 us
    unnamed x3, local copies, waits for them, and re-layouts  1.86 us

profile of v4, /device:TPU:1, one launch (start us, length us, event | category | flops | bytes accessed | tf_op | source)
XLA Modules:
  0.0 82.8 jit_solution(9627325752437700225)
XLA Ops:
  0.0 0.7 select_reduce_fusion.slots_ref
  0.7 0.0 copy-start
  0.8 0.9 %copy-done = bf16[128,384]{1,0:T(8,128)(2,1)S(1)} copy-done((bf16[128,384]{1,0:T(8,128)(2,1)S(1)}, bf16[128,384]{1,0:T(8,128)(2,1)}, u32[]{:S(2)}) %copy-start) | copy-done | bytes 98328
  1.6 80.2 %shard_map.37 = f32[128,2048]{1,0:T(8,128)S(1)} custom-call(s32[64]{0:T(128)S(1)} %select_reduce_fusion.slots_ref, bf16[40,128,128]{2,1,0:T(8,128)(2,1)} %bitcast.2, bf16[128,384]{1,0:T(8,128)(2,1)S(1)} %copy-done), custom_call_target="tpu_custom_call" | custom-call | flops 1700000000 | bytes 3000000 | tf_op jit(solution)/shard_map/pallas_call | solution.py:370
  81.8 1.0 %copy.5 = f32[128,2048]{1,0:T(8,128)} copy(f32[128,2048]{1,0:T(8,128)S(1)} %shard_map.37) | data formatting | bytes 2097152
  (1 shorter events, 0.0 us)
Async XLA Ops:
  0.7 0.9 %copy-start = (bf16[128,384]{1,0:T(8,128)(2,1)S(1)}, bf16[128,384]{1,0:T(8,128)(2,1)}, u32[]{:S(2)}) copy-start(bf16[128,384]{1,0:T(8,128)(2,1)} %occ_hbm.1) | copy-start | bytes 294916

commit v5 on v4

--- a/solution.py
+++ b/solution.py
@@ -11,11 +11,10 @@
 TILES = 40
 NY, NZ, NX = 4, 8, 4
 
-WINDOW = [(dz, dx, e) for dz in range(2) for dx in range(2) for e in range(2)]
+WINDOW = [(dz, e) for dz in range(2) for e in range(2)]
 ROWS = [(dx, e) for dx in range(NX) for e in range(2)]
-GROUPS = (((1, 2), (1, 1)), ((1, 3), (1, 0)), ((0, 2), (0, 1)), ((0, 3),), ((0, 0),))
-FIRST = (0, 2, 4, 6, 7)
-AHEAD = 5
+SERVED = (2, 1, 3, 0)
+GROUPS = [((j, k), (i, k)) for k in SERVED for j, i in ((2, 1), (3, 0))]
 CHUNKS = (0, 1, 2, 3)
 RELAYED = (0, 1)
 FORWARD = {2: 0, 3: 1}
@@ -23,9 +22,9 @@
 
 def greeted():
     out = set()
-    for dz, dx, e in WINDOW:
-        out.add((0, dz, dx, e))
-        out.add((0, -dz % NZ, -dx % NX, e))
+    for dz, e in WINDOW:
+        out.add((0, dz, 0, e))
+        out.add((0, -dz % NZ, 0, e))
     for dz in range(NZ):
         out.add((0, dz, 0, 0))
     for dy in range(NY):
@@ -38,7 +37,7 @@
 
 def kernel(
     slots_ref, tiles_hbm, occ_hbm, out_ref,
-    tiles_ref, dense, tiles_in, occ_in, part, part_in, mid, mid_in, rows, cols, pair, pair_in, done, done_in,
+    tiles_ref, dense, tiles_in, occ_in, own, part, part_in, mid, mid_in, rows, cols, pair, pair_in, done, done_in,
     mirror_in, relay, twin_in, twin, twin_done, twin_mirror,
     s_load, s_load_occ, s_tile, r_tile, s_occ, r_occ, s_part, r_part, s_mid, r_mid, s_row, r_row, s_col, r_col, s_pair, r_pair,
     s_done, r_done, s_mirror, r_mirror, s_relay, r_relay, s_twin, r_twin, s_out, r_out, s_back, r_back,
@@ -74,23 +73,23 @@
     shell_of = lambda zz: zz * (2 * NX) + x * 2 + c
     pl.semaphore_signal(barrier, inc=1, device_id=(zp, shell_of(other)), device_id_type=MESH)
 
-    def target(dz, dx, e):
+    def target(dz, e):
         tc = (c + e) % 2
         sign = 1 - 2 * tc
-        return (z - sign * dz + NZ) % NZ, (x - sign * dx + NX) % NX, tc
+        return (z - sign * dz + NZ) % NZ, x, tc
 
     def spread(g):
         for n, (j, k) in enumerate(GROUPS[g]):
 
-            def fill(s, carry, n=FIRST[g] + n, j=j, k=k):
-                tz, tx, tc = target(s // 4, (s // 2) % 2, s % 2)
-                block = ((tz + 2 * k) % NZ) * (2 * NX) + ((tx + 2 * j) % NX) * 2 + tc
+            def fill(s, carry, n=2 * g + n, j=j, k=k):
+                tz, tx, tc = target(s // 2, s % 2)
+                block = ((tz + 2 * k) % NZ) * (2 * NX) + ((tx + j) % NX) * 2 + tc
                 slot = slots_ref[block]
                 held = tiles_ref[jnp.maximum(slot - 1, 0)]
                 dense[s, n] = jnp.where(slot > 0, held, jnp.zeros_like(held))
                 return carry
 
-            lax.fori_loop(0, 8, fill, 0)
+            lax.fori_loop(0, len(WINDOW), fill, 0)
 
     load_occ.wait()
     pl.semaphore_wait(barrier, len(peers) + 1)
@@ -103,56 +102,60 @@
     arriving = {}
     load.wait()
 
-    def leave(g):
-        here = pl.ds(FIRST[g], len(GROUPS[g]))
+    for g in range(len(GROUPS)):
+        spread(g)
+        here = pl.ds(2 * g, 2)
         arriving[g] = []
         for s, w in enumerate(WINDOW):
             if s:
                 cp = copy(dense.at[s, here], tiles_in.at[s, here], s_tile.at[g, s], r_tile.at[g, s], device(0, *target(*w)))
                 cp.start()
                 arriving[g].append(cp)
-
-    for g in range(len(GROUPS)):
-        spread(g)
-        if g < AHEAD:
-            leave(g)
+        started += arriving[g]
     for cp in orbital:
         cp.wait_recv()
 
     facing = {}
     along = []
+
+    def add_up(k):
+        value = own[k]
+        for cp in facing[k]:
+            cp.wait_recv()
+        for j in range(1, NX):
+            value = value + part_in[k * NX + j].astype(jnp.float32)
+        if k == 0:
+            return value
+        mid[k] = value.astype(jnp.bfloat16)
+        cp = copy(mid.at[k], mid_in.at[k], s_mid.at[k], r_mid.at[k], near(0, 2 * k, 0, 0))
+        cp.start()
+        along.append((k, cp))
+        started.append(cp)
+
     for g, group in enumerate(GROUPS):
         for cp in arriving[g]:
             cp.wait_recv()
         lhs = jnp.concatenate(
             [
-                jnp.concatenate([dense[0, n]] + [tiles_in[s, n] for s in range(1, 8)], axis=1)
-                for n in range(FIRST[g], FIRST[g] + len(group))
+                jnp.concatenate([dense[0, n]] + [tiles_in[s, n] for s in range(1, len(WINDOW))], axis=1)
+                for n in (2 * g, 2 * g + 1)
             ],
             axis=0,
         )
-        both = jnp.dot(lhs, occ_in[...].reshape(8 * BLK, OCC), preferred_element_type=jnp.float32)
+        both = jnp.dot(lhs, occ_in[...].reshape(len(WINDOW) * BLK, OCC), preferred_element_type=jnp.float32)
         for n, (j, k) in enumerate(group):
             value = both[n * BLK:(n + 1) * BLK]
             if j:
-                part[k] = value.astype(jnp.bfloat16)
-                cp = copy(part.at[k], part_in.at[k], s_part.at[k], r_part.at[k], near(0, 0, 2, 0))
-                facing[k] = cp
+                i = k * NX + j
+                part[i] = value.astype(jnp.bfloat16)
+                cp = copy(part.at[i], part_in.at[i], s_part.at[i], r_part.at[i], near(0, 0, j, 0))
+                cp.start()
+                facing.setdefault(k, []).append(cp)
+                started.append(cp)
             else:
-                facing[k].wait_recv()
-                value = value + part_in[k].astype(jnp.float32)
-                if k == 0:
-                    total = value
-                    continue
-                mid[k] = value.astype(jnp.bfloat16)
-                cp = copy(mid.at[k], mid_in.at[k], s_mid.at[k], r_mid.at[k], near(0, 2 * k, 0, 0))
-                along.append((k, cp))
-            cp.start()
-            started.append(cp)
-        for cp in arriving[g]:
-            cp.wait_send()
-        if g + AHEAD < len(GROUPS):
-            leave(g + AHEAD)
+                own[k] = value
+    for k in SERVED:
+        total = add_up(k)
     for k, cp in along:
         cp.wait_recv()
         total = total + mid_in[k].astype(jnp.float32)
@@ -374,11 +377,12 @@
         out_specs=pl.BlockSpec(memory_space=pltpu.VMEM),
         scratch_shapes=[
             pltpu.VMEM((TILES, BLK, BLK), bf16),
-            pltpu.VMEM((8, 8, BLK, BLK), bf16),
-            pltpu.VMEM((8, 8, BLK, BLK), bf16),
-            pltpu.VMEM((8, BLK, OCC), bf16),
+            pltpu.VMEM((4, 16, BLK, BLK), bf16),
+            pltpu.VMEM((4, 16, BLK, BLK), bf16),
             pltpu.VMEM((4, BLK, OCC), bf16),
-            pltpu.VMEM((4, BLK, OCC), bf16),
+            pltpu.VMEM((4, BLK, OCC), f32),
+            pltpu.VMEM((16, BLK, OCC), bf16),
+            pltpu.VMEM((16, BLK, OCC), bf16),
             pltpu.VMEM((4, BLK, OCC), bf16),
             pltpu.VMEM((4, BLK, OCC), bf16),
             pltpu.VMEM((8, BLK, OCC), bf16),
@@ -394,7 +398,7 @@
             pltpu.VMEM((4, BLK, BLK), bf16),
             pltpu.VMEM((4, BLK, BLK), bf16),
             dma(()), dma(()),
-            dma((5, 8)), dma((5, 8)), dma((8,)), dma((8,)), dma((4,)), dma((4,)), dma((4,)), dma((4,)),
+            dma((8, 4)), dma((8, 4)), dma((4,)), dma((4,)), dma((16,)), dma((16,)), dma((4,)), dma((4,)),
             dma((8,)), dma((8,)), dma((4,)), dma((4,)), dma((4, 4)), dma((4, 4)),
             dma((8,)), dma((8,)), dma((4,)), dma((4,)), dma((4, 2)), dma((4, 2)), dma(()), dma((4,)), dma((4,)), dma((4,)), dma(()), dma(()),
         ],

time: 82.9 us -> 78.8 us (0.951)
  Pallas kernels: 80.2 us -> 76.1 us
    pallas_call x1, Pallas kernels: 80.2 us -> 76.1 us  [body(): pl.pallas_call(kernel, out_shape=jax.ShapeDtypeStruct((BLK, 2048), f32),...]
where the time goes in v5:
time: 78.8 us; the launch traced here: 78.7 us
  Pallas kernels  76.1 us (97%)
  local copies, waits for them, and re-layouts  1.86 us (2%)
    pallas_call x1, Pallas kernels, body(): pl.pallas_call(kernel, out_shape=jax.ShapeDtypeStruct((BLK, 2048), f32),...  76.1 us
    unnamed x3, local copies, waits for them, and re-layouts  1.86 us

profile of v5, /device:TPU:1, one launch (start us, length us, event | category | flops | bytes accessed | tf_op | source)
XLA Modules:
  0.0 78.7 jit_solution(5051826535481104021)
XLA Ops:
  0.0 0.7 select_reduce_fusion.slots_ref
  0.7 0.0 copy-start
  0.8 0.9 %copy-done = bf16[128,384]{1,0:T(8,128)(2,1)S(1)} copy-done((bf16[128,384]{1,0:T(8,128)(2,1)S(1)}, bf16[128,384]{1,0:T(8,128)(2,1)}, u32[]{:S(2)}) %copy-start) | copy-done | bytes 98328
  1.6 76.1 %shard_map.37 = f32[128,2048]{1,0:T(8,128)S(1)} custom-call(s32[64]{0:T(128)S(1)} %select_reduce_fusion.slots_ref, bf16[40,128,128]{2,1,0:T(8,128)(2,1)} %bitcast.2, bf16[128,384]{1,0:T(8,128)(2,1)S(1)} %copy-done), custom_call_target="tpu_custom_call" | custom-call | flops 1700000000 | bytes 3000000 | tf_op jit(solution)/shard_map/pallas_call | solution.py:373
  77.7 1.0 %copy.5 = f32[128,2048]{1,0:T(8,128)} copy(f32[128,2048]{1,0:T(8,128)S(1)} %shard_map.37) | data formatting | bytes 2097152
  (1 shorter events, 0.0 us)
Async XLA Ops:
  0.7 0.9 %copy-start = (bf16[128,384]{1,0:T(8,128)(2,1)S(1)}, bf16[128,384]{1,0:T(8,128)(2,1)}, u32[]{:S(2)}) copy-start(bf16[128,384]{1,0:T(8,128)(2,1)} %occ_hbm.1) | copy-start | bytes 294916

commit v6 on v5

--- a/solution.py
+++ b/solution.py
@@ -12,9 +12,14 @@
 NY, NZ, NX = 4, 8, 4
 
 WINDOW = [(dz, e) for dz in range(2) for e in range(2)]
+OFFSET = (0, -2, 3, 1)
+AFTER, HERE, BEFORE = 0, 2, 4
 ROWS = [(dx, e) for dx in range(NX) for e in range(2)]
-SERVED = (2, 1, 3, 0)
-GROUPS = [((j, k), (i, k)) for k in SERVED for j, i in ((2, 1), (3, 0))]
+SERVED = (2, 3, 1, 0)
+GROUPS = (
+    ((2, 2), (2, 3)), ((2, 1), (2, 0)), ((3, 2), (3, 3)), ((1, 2), (1, 3)),
+    ((1, 1), (3, 1)), ((3, 0), (1, 0)), ((0, 2), (0, 3)), ((0, 1), (0, 0)),
+)
 CHUNKS = (0, 1, 2, 3)
 RELAYED = (0, 1)
 FORWARD = {2: 0, 3: 1}
@@ -60,7 +65,7 @@
     started = []
     load = pltpu.make_async_copy(tiles_hbm, tiles_ref, s_load)
     load.start()
-    load_occ = pltpu.make_async_copy(occ_hbm, occ_in.at[0], s_load_occ)
+    load_occ = pltpu.make_async_copy(occ_hbm, occ_in.at[HERE], s_load_occ)
     load_occ.start()
     peers = greeted()
     barrier = pltpu.get_barrier_semaphore()
@@ -73,17 +78,20 @@
     shell_of = lambda zz: zz * (2 * NX) + x * 2 + c
     pl.semaphore_signal(barrier, inc=1, device_id=(zp, shell_of(other)), device_id_type=MESH)
 
-    def target(dz, e):
+    sign = 1 - 2 * c
+
+    def target(dz, e, k):
         tc = (c + e) % 2
-        sign = 1 - 2 * tc
-        return (z - sign * dz + NZ) % NZ, x, tc
+        toward = (1 - 2 * tc) * (-1 if k < 2 else 1)
+        return (z + toward * dz + NZ) % NZ, x, tc
 
     def spread(g):
         for n, (j, k) in enumerate(GROUPS[g]):
 
             def fill(s, carry, n=2 * g + n, j=j, k=k):
-                tz, tx, tc = target(s // 2, s % 2)
-                block = ((tz + 2 * k) % NZ) * (2 * NX) + ((tx + j) % NX) * 2 + tc
+                tz, tx, tc = target(s // 2, s % 2, k)
+                owner = (tz + (1 - 2 * tc) * OFFSET[k] + NZ) % NZ
+                block = owner * (2 * NX) + ((tx + (1 - 2 * tc) * j + NX) % NX) * 2 + tc
                 slot = slots_ref[block]
                 held = tiles_ref[jnp.maximum(slot - 1, 0)]
                 dense[s, n] = jnp.where(slot > 0, held, jnp.zeros_like(held))
@@ -93,11 +101,16 @@
 
     load_occ.wait()
     pl.semaphore_wait(barrier, len(peers) + 1)
-    for s, w in enumerate(WINDOW):
-        if s:
-            cp = copy(occ_in.at[0], occ_in.at[s], s_occ.at[s], r_occ.at[s], device(0, *target(*w)))
-            cp.start()
-            started.append(cp)
+    def orbit(slot, to_slot, to):
+        return copy(occ_in.at[slot], occ_in.at[to_slot], s_occ.at[to_slot], r_occ.at[to_slot], to)
+
+    mate = near(0, 0, 0, 1)
+    onward = device(0, (z + sign + NZ) % NZ, x, c)
+    backward = device(0, (z - sign + NZ) % NZ, x, c)
+    for to_slot, to in ((AFTER, backward), (BEFORE, onward), (HERE + 1, mate)):
+        cp = orbit(HERE, to_slot, to)
+        cp.start()
+        started.append(cp)
     orbital = list(started)
     arriving = {}
     load.wait()
@@ -108,26 +121,33 @@
         arriving[g] = []
         for s, w in enumerate(WINDOW):
             if s:
-                cp = copy(dense.at[s, here], tiles_in.at[s, here], s_tile.at[g, s], r_tile.at[g, s], device(0, *target(*w)))
+                cp = copy(dense.at[s, here], tiles_in.at[s, here], s_tile.at[g, s], r_tile.at[g, s], device(0, *target(*w, GROUPS[g][0][1])))
                 cp.start()
                 arriving[g].append(cp)
         started += arriving[g]
-    for cp in orbital:
+    for cp, to_slot in zip(orbital, (BEFORE + 1, AFTER + 1)):
         cp.wait_recv()
+        cp = orbit(BEFORE + AFTER - to_slot + 1, to_slot, mate)
+        cp.start()
+        started.append(cp)
+        orbital.append(cp)
+    for cp in orbital[2:]:
+        cp.wait_recv()
 
     facing = {}
+    passing = {}
     along = []
 
     def add_up(k):
         value = own[k]
         for cp in facing[k]:
             cp.wait_recv()
-        for j in range(1, NX):
+        for j in (1, 3):
             value = value + part_in[k * NX + j].astype(jnp.float32)
         if k == 0:
             return value
         mid[k] = value.astype(jnp.bfloat16)
-        cp = copy(mid.at[k], mid_in.at[k], s_mid.at[k], r_mid.at[k], near(0, 2 * k, 0, 0))
+        cp = copy(mid.at[k], mid_in.at[k], s_mid.at[k], r_mid.at[k], device(0, (z + sign * OFFSET[k] + NZ) % NZ, x, c))
         cp.start()
         along.append((k, cp))
         started.append(cp)
@@ -142,19 +162,32 @@
             ],
             axis=0,
         )
-        both = jnp.dot(lhs, occ_in[...].reshape(len(WINDOW) * BLK, OCC), preferred_element_type=jnp.float32)
+        order = (HERE, HERE + 1, AFTER, AFTER + 1) if group[0][1] < 2 else (HERE, HERE + 1, BEFORE, BEFORE + 1)
+        rhs = jnp.concatenate([occ_in[i] for i in order], axis=0)
+        both = jnp.dot(lhs, rhs, preferred_element_type=jnp.float32)
         for n, (j, k) in enumerate(group):
             value = both[n * BLK:(n + 1) * BLK]
             if j:
                 i = k * NX + j
+                if j == 1:
+                    passing[k].wait_recv()
+                    value = value + part_in[k * NX + 2].astype(jnp.float32)
                 part[i] = value.astype(jnp.bfloat16)
-                cp = copy(part.at[i], part_in.at[i], s_part.at[i], r_part.at[i], near(0, 0, j, 0))
+                step = -sign if j == 3 else sign
+                to = device(0, z, (x + step + NX) % NX, c)
+                cp = copy(part.at[i], part_in.at[i], s_part.at[i], r_part.at[i], to)
                 cp.start()
-                facing.setdefault(k, []).append(cp)
                 started.append(cp)
+                if j == 2:
+                    passing[k] = cp
+                else:
+                    facing.setdefault(k, []).append(cp)
             else:
                 own[k] = value
-    for k in SERVED:
+        if g == 6:
+            for k in SERVED[:2]:
+                add_up(k)
+    for k in SERVED[2:]:
         total = add_up(k)
     for k, cp in along:
         cp.wait_recv()
@@ -379,7 +412,7 @@
             pltpu.VMEM((TILES, BLK, BLK), bf16),
             pltpu.VMEM((4, 16, BLK, BLK), bf16),
             pltpu.VMEM((4, 16, BLK, BLK), bf16),
-            pltpu.VMEM((4, BLK, OCC), bf16),
+            pltpu.VMEM((6, BLK, OCC), bf16),
             pltpu.VMEM((4, BLK, OCC), f32),
             pltpu.VMEM((16, BLK, OCC), bf16),
             pltpu.VMEM((16, BLK, OCC), bf16),
@@ -398,7 +431,7 @@
             pltpu.VMEM((4, BLK, BLK), bf16),
             pltpu.VMEM((4, BLK, BLK), bf16),
             dma(()), dma(()),
-            dma((8, 4)), dma((8, 4)), dma((4,)), dma((4,)), dma((16,)), dma((16,)), dma((4,)), dma((4,)),
+            dma((8, 4)), dma((8, 4)), dma((6,)), dma((6,)), dma((16,)), dma((16,)), dma((4,)), dma((4,)),
             dma((8,)), dma((8,)), dma((4,)), dma((4,)), dma((4, 4)), dma((4, 4)),
             dma((8,)), dma((8,)), dma((4,)), dma((4,)), dma((4, 2)), dma((4, 2)), dma(()), dma((4,)), dma((4,)), dma((4,)), dma(()), dma(()),
         ],

time: 78.8 us -> 77.9 us (0.989)
  Pallas kernels: 76.1 us -> 75.1 us
    pallas_call x1, Pallas kernels: 76.1 us -> 75.1 us  [body(): pl.pallas_call(kernel, out_shape=jax.ShapeDtypeStruct((BLK, 2048), f32),...]
where the time goes in v6:
time: 77.9 us; the launch traced here: 77.8 us
  Pallas kernels  75.1 us (96%)
  local copies, waits for them, and re-layouts  1.86 us (2%)
    pallas_call x1, Pallas kernels, body(): pl.pallas_call(kernel, out_shape=jax.ShapeDtypeStruct((BLK, 2048), f32),...  75.1 us
    unnamed x3, local copies, waits for them, and re-layouts  1.86 us

profile of v6, /device:TPU:1, one launch (start us, length us, event | category | flops | bytes accessed | tf_op | source)
XLA Modules:
  0.0 77.8 jit_solution(13556206530915965265)
XLA Ops:
  0.0 0.7 select_reduce_fusion.slots_ref
  0.7 0.0 copy-start
  0.8 0.9 %copy-done = bf16[128,384]{1,0:T(8,128)(2,1)S(1)} copy-done((bf16[128,384]{1,0:T(8,128)(2,1)S(1)}, bf16[128,384]{1,0:T(8,128)(2,1)}, u32[]{:S(2)}) %copy-start) | copy-done | bytes 98328
  1.6 75.1 %shard_map.37 = f32[128,2048]{1,0:T(8,128)S(1)} custom-call(s32[64]{0:T(128)S(1)} %select_reduce_fusion.slots_ref, bf16[40,128,128]{2,1,0:T(8,128)(2,1)} %bitcast.2, bf16[128,384]{1,0:T(8,128)(2,1)S(1)} %copy-done), custom_call_target="tpu_custom_call" | custom-call | flops 1700000000 | bytes 3000000 | tf_op jit(solution)/shard_map/pallas_call | solution.py:406
  76.8 1.0 %copy.5 = f32[128,2048]{1,0:T(8,128)} copy(f32[128,2048]{1,0:T(8,128)S(1)} %shard_map.37) | data formatting | bytes 2097152
  (1 shorter events, 0.0 us)
Async XLA Ops:
  0.7 0.9 %copy-start = (bf16[128,384]{1,0:T(8,128)(2,1)S(1)}, bf16[128,384]{1,0:T(8,128)(2,1)}, u32[]{:S(2)}) copy-start(bf16[128,384]{1,0:T(8,128)(2,1)} %occ_hbm.1) | copy-start | bytes 294916

commit v7 on v6

--- a/solution.py
+++ b/solution.py
@@ -203,7 +203,7 @@
         cp.start()
         across[r] = cp
         started.append(cp)
-    for d in (2, 1, 3, 0):
+    for d in (1, 3, 2, 0):
         there = (zp + d) % 4
         if d:
             tz = 2 * there + jnp.where(there < zp, zs, 1 - zs)
@@ -249,7 +249,7 @@
         for a in range(5):
             for i in range(2):
                 pair[a, 2 * q + i] = block[i * BLK:(i + 1) * BLK, a * BLK:(a + 1) * BLK]
-        for dy in (2, 1, 3):
+        for dy in (1, 3, 2):
             share(dy, q).start()
 
     half = pl.ds(2 * zs, 4)
@@ -303,6 +303,9 @@
 
     for q in range(4):
         issue(q)
+        if q == 3:
+            while started:
+                started.pop().wait_send()
         if q == 2:
             @pl.when(jnp.logical_not(home))
             def _():

time: 77.9 us -> 75.4 us (0.968); the launches traced: 77.8 us -> 74.2 us
  Pallas kernels: 75.1 us -> 71.5 us
    pallas_call x1, Pallas kernels: 75.1 us -> 71.5 us  [body(): pl.pallas_call(kernel, out_shape=jax.ShapeDtypeStruct((BLK, 2048), f32),...]
where the time goes in v7:
time: 75.4 us; the launch traced here: 74.2 us
  Pallas kernels  71.5 us (95%)
  local copies, waits for them, and re-layouts  1.86 us (2%)
    pallas_call x1, Pallas kernels, body(): pl.pallas_call(kernel, out_shape=jax.ShapeDtypeStruct((BLK, 2048), f32),...  71.5 us
    unnamed x3, local copies, waits for them, and re-layouts  1.86 us

profile of v7, /device:TPU:1, one launch (start us, length us, event | category | flops | bytes accessed | tf_op | source)
XLA Modules:
  0.0 74.2 jit_solution(104633166942296231)
XLA Ops:
  0.0 0.7 %select_reduce_fusion.slots_ref = s32[64]{0:T(128)S(1)} fusion(s32[40]{0:T(128)S(1)} %iota_add_fusion, s32[40]{0:T(128)} %bitcast.3), kind=kLoop, calls=%fused_computation | loop fusion | flops 7616 | bytes 576 | tf_op jit(solution)/shard_map/reduce_sum | solution.py:405
  0.7 0.0 copy-start
  0.8 0.9 %copy-done = bf16[128,384]{1,0:T(8,128)(2,1)S(1)} copy-done((bf16[128,384]{1,0:T(8,128)(2,1)S(1)}, bf16[128,384]{1,0:T(8,128)(2,1)}, u32[]{:S(2)}) %copy-start) | copy-done | bytes 98328
  1.6 71.5 %shard_map.37 = f32[128,2048]{1,0:T(8,128)S(1)} custom-call(s32[64]{0:T(128)S(1)} %select_reduce_fusion.slots_ref, bf16[40,128,128]{2,1,0:T(8,128)(2,1)} %bitcast.2, bf16[128,384]{1,0:T(8,128)(2,1)S(1)} %copy-done), custom_call_target="tpu_custom_call" | custom-call | flops 1700000000 | bytes 3000000 | tf_op jit(solution)/shard_map/pallas_call | solution.py:409
  73.2 1.0 %copy.5 = f32[128,2048]{1,0:T(8,128)} copy(f32[128,2048]{1,0:T(8,128)S(1)} %shard_map.37) | data formatting | bytes 2097152
  (1 shorter events, 0.0 us)
Async XLA Ops:
  0.7 0.9 %copy-start = (bf16[128,384]{1,0:T(8,128)(2,1)S(1)}, bf16[128,384]{1,0:T(8,128)(2,1)}, u32[]{:S(2)}) copy-start(bf16[128,384]{1,0:T(8,128)(2,1)} %occ_hbm.1) | copy-start | bytes 294916
